TPU v7x, 32 devices: a whole 2x2x4 slice. The times are simulated.
32 devices in a mesh: lib: 8 (over z, y), lmk: 4 (over x, core).
Axes of the slice: x: 2, y: 2, z: 4, core: 2. Of those that a mesh axis runs over, the one named last changes fastest.
Arguments:
- library_bits: bfloat16 [6144, 2048], P('lib'), may hold values from 0 to 1, as said below
- library_count: int32 [6144], P('lib'), may hold values from 1 to 2048, as said below
- landmark_bits: bfloat16 [8192, 2048], P('lmk'), may hold values from 0 to 1, as said below
- landmark_count: int32 [8192], P('lmk'), may hold values from 1 to 2048, as said below
- inverse_root: bfloat16 [8192, 8192], P('lib', 'lmk'), may hold values from -0.09375 to 0.09375
Outputs:
- features: float32 [6144, 8192], P('lib', 'lmk')
Inputs may be any that keep to these rules, and one draw needn't show every extreme that they name: `library_bits`: every entry is 0 or 1; every fingerprint has at least one set bit, one has all 2048 set and one has exactly one. `library_count`: the number of ones in the same row of library_bits. `landmark_bits`: every entry is 0 or 1; every fingerprint has at least one set bit, one has all 2048 set and one has exactly one. `landmark_count`: the number of ones in the same row of landmark_bits.
All inputs are finite; a program needn't handle non-finite values.
Results may differ from a plain program's by a relative error of at most 0.0027.
Values may be sent and summed in bfloat16 or wider, within the bound.
A program may use at most 128 MiB of HBM per device.

v0:
```python
import jax
import jax.numpy as jnp
from jax import lax
from jax.sharding import PartitionSpec as P


def tversky(row_bits, row_count, col_bits, col_count):
    common = lax.dot_general(
        row_bits, col_bits, (((1,), (1,)), ((), ())), preferred_element_type=jnp.float32
    )
    scale_sum = (
        0.9 * row_count.astype(jnp.float32)[:, None] + 0.1 * col_count.astype(jnp.float32)[None, :]
    )
    return (common / scale_sum).astype(jnp.bfloat16)


def shards(library_bits, library_count, landmark_bits, landmark_count, inverse_root):
    block = tversky(library_bits, library_count, landmark_bits, landmark_count)
    row_kernel = lax.all_gather(block, "lmk", axis=1, tiled=True)
    return jnp.dot(
        row_kernel,
        lax.all_gather(inverse_root, "lib", axis=0, tiled=True),
        preferred_element_type=jnp.float32,
    )


def solution(mesh):
    placed = (P("lib", None), P("lib"), P("lmk", None), P("lmk"), P("lib", "lmk"))
    return jax.shard_map(
        shards, mesh=mesh, in_specs=placed, out_specs=P("lib", "lmk"), check_vma=False
    )
```

profile of v0, /device:TPU:17, one launch (start us, length us, event | category | flops | bytes accessed | tf_op | source)
XLA Modules:
  0.0 782.2 jit_solution(5418699888149935171)
XLA Ops:
  6.5 0.0 copy-start
  6.5 0.0 all-gather.3.cloned.1.call-start
  6.5 0.8 convert_multiply_fusion.1
  7.4 0.8 convert_multiply_fusion
  8.2 0.2 copy-done
  8.4 10.3 %divide_convert_fusion = bf16[768,2048]{1,0:T(8,128)(2,1)} fusion(bf16[768,2048]{1,0:T(8,128)(2,1)S(1)} %copy-done, bf16[2048,2048]{1,0:T(8,128)(2,1)} %param.7, f32[2048]{0:T(1024)S(1)} %convert_multiply_fusion, f32[768]{0:T(1024)S(1)} %convert_multiply_fusion.1), kind=kOutput, calls=%fused_computation | convolution fusion | flops 6447169536 | bytes 14691328 | tf_op jit(solution)/shard_map/dot_general | solution.py:8
  18.7 0.0 all-gather.3.cloned.1.call-update
  18.7 0.0 all-gather.5.cloned.1.call-start
  18.8 0.7 all-gather.5.cloned.1.call-update
  19.5 83.0 %all-gather.3.cloned.1.call-done = bf16[768,8192]{1,0:T(8,128)(2,1)} async-done(((bf16[768,2048]{1,0:T(8,128)(2,1)}), bf16[768,8192]{1,0:T(8,128)(2,1)}) %all-gather.3.cloned.1.call-update) | async-done | bytes 12582928 | tf_op jit(solution)/shard_map/all_gather | solution.py:19
  102.5 639.1 %all-gather.5.cloned.1.call-done = bf16[8192,2048]{1,0:T(8,128)(2,1)} async-done(((bf16[1024,2048]{1,0:T(8,128)(2,1)}), bf16[8192,2048]{1,0:T(8,128)(2,1)}) %all-gather.5.cloned.1.call-update) | async-done | bytes 33554448 | tf_op jit(solution)/shard_map/all_gather | solution.py:22
  741.5 0.0 copy-start.1
  741.5 33.8 %fusion = f32[768,2048]{1,0:T(8,128)} fusion(bf16[768,8192]{1,0:T(8,128)(2,1)} %all-gather.3.cloned.1.call-done, bf16[8192,2048]{1,0:T(8,128)(2,1)} %all-gather.5.cloned.1.call-done), kind=kOutput, calls=%fused_computation.3 | convolution fusion | flops 25769803776 | bytes 52428800 | tf_op jit(solution)/shard_map/dot_general | solution.py:20
  775.4 0.0 copy-done.1
Async XLA Ops:
  6.5 1.9 copy-start
  6.5 95.9 %all-gather.3.cloned.1.call-start = ((), (), s32[]{:S(2)}) async-start(), calls=%async_computation | async-start | bytes 15728640 | tf_op jit(solution)/shard_map/all_gather | solution.py:19
  18.7 722.8 %all-gather.5.cloned.1.call-start = ((), (), s32[]{:S(2)}) async-start(), calls=%async_computation.1 | async-start | bytes 37748736 | tf_op jit(solution)/shard_map/all_gather | solution.py:22
  741.5 33.8 %copy-start.1 = (bf16[768,2048]{1,0:T(8,128)(2,1)S(1)}, bf16[768,2048]{1,0:T(8,128)(2,1)}, u32[]{:S(2)}) copy-start(bf16[768,2048]{1,0:T(8,128)(2,1)} %param.5) | copy-start | bytes 9437188
Sparse Core Ops, SparseCore 0:
  18.8 83.5 all-gather.2
  104.0 637.4 all-gather.4
where the time goes:
time: 784 us; the launch traced here: 782 us
  waiting for transfers between devices  723 us (92%)
  matrix products  44.1 us (6%)
  between operations  13.4 us (2%)
    all_gather x1, waiting for transfers between devices, shards(): lax.all_gather(inverse_root, 'lib', axis=0, tiled=True)  639 us
    all_gather x1, waiting for transfers between devices, shards(): row_kernel = lax.all_gather(block, 'lmk', axis=1, tiled=True)  83 us
    dot_general x1, matrix products, shards(): jnp.dot(row_kernel, lax.all_gather(inverse_root, 'lib', axis=0, tiled=Tru...  33.8 us
  transfers between devices with their start and end apart: 2, of which 2 were waited for; matrix products, arithmetic and copies ran while one was open for 0% of the time, Pallas kernels for 0%

commit v1 on v0

v1 whole, which is shorter than its diff:
```python
import jax
import jax.numpy as jnp
from jax import lax
from jax.sharding import PartitionSpec as P

DEPTH = 4


def tversky(row_bits, row_count, col_bits, col_count):
    common = lax.dot_general(
        row_bits, col_bits, (((1,), (1,)), ((), ())), preferred_element_type=jnp.float32
    )
    scale_sum = (
        0.9 * row_count.astype(jnp.float32)[:, None] + 0.1 * col_count.astype(jnp.float32)[None, :]
    )
    return (common / scale_sum).astype(jnp.bfloat16)


def split_sum(n_lib, n_lmk, library_bits, library_count, landmark_bits, landmark_count, inverse_root):
    layer = n_lib // DEPTH
    swap = [(i, i ^ layer) for i in range(n_lib)]
    parity = (lax.axis_index("lib") // layer) % 2
    groups = [[i for i in range(n_lib) if (i // layer) % 2 == p] for p in (0, 1)]
    root = lax.all_gather(inverse_root, "lib", axis=0, tiled=True, axis_index_groups=groups)

    rows = library_bits.shape[0]
    other_bits = lax.ppermute(library_bits, "lib", swap)
    other_count = lax.ppermute(library_count, "lib", swap)
    block = tversky(
        jnp.concatenate([other_bits, library_bits]),
        jnp.concatenate([other_count, library_count]),
        landmark_bits,
        landmark_count,
    )
    kernel = lax.all_gather(block, "lmk", axis=1, tiled=True)
    quarter = kernel.shape[1] // DEPTH
    half = jnp.concatenate(
        [lax.dynamic_slice_in_dim(kernel, (2 * k + parity) * quarter, quarter, 1) for k in (0, 1)], 1
    )
    theirs = jnp.dot(half[:rows], root, preferred_element_type=jnp.float32).astype(jnp.bfloat16)
    arrived = lax.ppermute(theirs, "lib", swap)
    mine = jnp.dot(half[rows:], root, preferred_element_type=jnp.float32)
    return mine + arrived.astype(jnp.float32)


def solution(mesh):
    placed = (P("lib", None), P("lib"), P("lmk", None), P("lmk"), P("lib", "lmk"))
    n_lib, n_lmk = mesh.shape["lib"], mesh.shape["lmk"]

    def shards(*blocks):
        return split_sum(n_lib, n_lmk, *blocks)

    return jax.shard_map(
        shards, mesh=mesh, in_specs=placed, out_specs=P("lib", "lmk"), check_vma=False
    )
```

time: 784 us -> 666 us (0.85)
  waiting for transfers between devices: 723 us -> 570 us
  matrix products: 44.1 us -> 58.5 us
  local copies, waits for them, and re-layouts: 0.25 us -> 14 us
    all_gather x2, waiting for transfers between devices: 722 us -> 434 us  [the longest x1 277 us: split_sum(): lax.all_gather(inverse_root, 'lib', axis=0, tiled=True, axis_index_groups...]
    ppermute x0 -> x3, waiting for transfers between devices: none -> 135 us  [the longest x1 68.2 us: split_sum(): arrived = lax.ppermute(theirs, 'lib', swap)]
    dynamic_slice x0 -> x1, local copies, waits for them, and re-layouts: none -> 14 us  [split_sum(): lax.dynamic_slice_in_dim(kernel, (2 * k + parity) * quarter, quarter, 1)]
    dot_general x1, matrix products: 10.3 us -> 18.6 us  [tversky(): lax.dot_general(row_bits, col_bits, (((1,), (1,)), ((), ())), preferred_e...]
    dot_general x1 -> x2, matrix products: 33.8 us -> 39.8 us  [the longest x1 21 us: split_sum(): jnp.dot(half[:rows], root, preferred_element_type=jnp.float32)]
  transfers between devices with their start and end apart: 2 -> 5, of which waited for: 2 -> 4; matrix products, arithmetic and copies ran while one was open for 0% -> 2% of each run, Pallas kernels for 0% -> 0%
where the time goes in v1:
time: 666 us; the launch traced here: 661 us
  waiting for transfers between devices  570 us (86%)
  matrix products  58.5 us (9%)
  local copies, waits for them, and re-layouts  14 us (2%)
  between operations  13.5 us (2%)
    all_gather x1, waiting for transfers between devices, split_sum(): lax.all_gather(inverse_root, 'lib', axis=0, tiled=True, axis_index_groups...  277 us
    all_gather x1, waiting for transfers between devices, split_sum(): kernel = lax.all_gather(block, 'lmk', axis=1, tiled=True)  157 us
    ppermute x1, waiting for transfers between devices, split_sum(): arrived = lax.ppermute(theirs, 'lib', swap)  68.2 us
    ppermute x1, waiting for transfers between devices, split_sum(): other_count = lax.ppermute(library_count, 'lib', swap)  67.1 us
    dot_general x1, matrix products, split_sum(): jnp.dot(half[:rows], root, preferred_element_type=jnp.float32)  21 us
    dot_general x1, matrix products, split_sum(): mine = jnp.dot(half[rows:], root, preferred_element_type=jnp.float32)  18.8 us
    dot_general x1, matrix products, tversky(): lax.dot_general(row_bits, col_bits, (((1,), (1,)), ((), ())), preferred_e...  18.6 us
    dynamic_slice x1, local copies, waits for them, and re-layouts, split_sum(): lax.dynamic_slice_in_dim(kernel, (2 * k + parity) * quarter, quarter, 1)  14 us
  transfers between devices with their start and end apart: 5, of which 4 were waited for; matrix products, arithmetic and copies ran while one was open for 2% of the time, Pallas kernels for 0%

profile of v1, /device:TPU:17, one launch (start us, length us, event | category | flops | bytes accessed | tf_op | source)
XLA Modules:
  0.0 661.3 jit_solution(11303867675992590488)
XLA Ops:
  6.5 0.0 all-gather.3.cloned.1.call-start
  6.5 1.3 collective-permute-start
  7.8 0.2 collective-permute-start.1
  8.0 0.7 convert_multiply_fusion
  8.7 67.1 %collective-permute-done.1 = s32[768]{0:T(1024)S(1)} collective-permute-done((s32[768]{0:T(1024)}, s32[768]{0:T(1024)S(1)}, u32[]{:S(2)}, u32[]{:S(2)}) %collective-permute-start.1) | collective-permute-done | bytes 3104 | tf_op jit(solution)/shard_map/ppermute | solution.py:28
  75.8 0.7 fusion.9
  76.5 0.0 collective-permute-done
  76.5 18.6 %divide_convert_fusion = bf16[1536,2048]{1,0:T(8,128)(2,1)} fusion(bf16[2048,2048]{1,0:T(8,128)(2,1)} %param.7, bf16[768,2048]{1,0:T(8,128)(2,1)} %param.5, bf16[768,2048]{1,0:T(8,128)(2,1)S(1)} %collective-permute-done, f32[2048]{0:T(1024)S(1)} %convert_multiply_fusion, f32[1536]{0:T(1024)S(1)} %fusion.9), kind=kOutput, calls=%fused_computation.2 | convolution fusion | flops 12906921984 | bytes 20985856 | tf_op jit(solution)/shard_map/dot_general | solution.py:10
  95.2 0.0 all-gather.3.cloned.1.call-update
  95.2 0.2 all-gather.5.cloned.1.call-start
  95.4 0.5 all-gather.5.cloned.1.call-update
  96.0 156.5 %all-gather.3.cloned.1.call-done = bf16[1536,8192]{1,0:T(8,128)(2,1)} async-done(((bf16[1536,2048]{1,0:T(8,128)(2,1)}), bf16[1536,8192]{1,0:T(8,128)(2,1)}) %all-gather.3.cloned.1.call-update) | async-done | bytes 25165840 | tf_op jit(solution)/shard_map/all_gather | solution.py:35
  252.5 14.0 %constant_dynamic-slice_fusion.1 = (bf16[1536,2048]{1,0:T(8,128)(2,1)}, bf16[1536,2048]{1,0:T(8,128)(2,1)}) fusion(bf16[1536,8192]{1,0:T(8,128)(2,1)} %all-gather.3.cloned.1.call-done, s32[]{:T(128)S(6)} %select_n.19, s32[]{:T(128)S(6)} %select_n.20), kind=kLoop, calls=%fused_computation.17 | loop fusion | bytes 25165832 | tf_op jit(solution)/shard_map/dynamic_slice | solution.py:38
  266.5 277.5 %all-gather.5.cloned.1.call-done = bf16[4096,2048]{1,0:T(8,128)(2,1)} async-done(((bf16[1024,2048]{1,0:T(8,128)(2,1)}), bf16[4096,2048]{1,0:T(8,128)(2,1)}) %all-gather.5.cloned.1.call-update) | async-done | bytes 16777232 | tf_op jit(solution)/shard_map/all_gather | solution.py:24
  544.0 0.0 copy-start
  544.0 0.0 copy-start.1
  544.0 21.0 %fusion.8 = bf16[768,2048]{1,0:T(8,128)(2,1)S(1)} fusion(bf16[4096,2048]{1,0:T(8,128)(2,1)} %all-gather.5.cloned.1.call-done, bf16[1536,2048]{1,0:T(8,128)(2,1)} %get-tuple-element.6, bf16[1536,2048]{1,0:T(8,128)(2,1)} %get-tuple-element.5), kind=kOutput, calls=%fused_computation.12 | convolution fusion | flops 12899057664 | bytes 32505856 | tf_op jit(solution)/shard_map/dot_general | solution.py:40
  565.0 2.4 collective-permute-start.2
  567.4 68.2 %collective-permute-done.2 = bf16[768,2048]{1,0:T(8,128)(2,1)} collective-permute-done((bf16[768,2048]{1,0:T(8,128)(2,1)S(1)}, bf16[768,2048]{1,0:T(8,128)(2,1)}, u32[]{:S(2)}, u32[]{:S(2)}) %collective-permute-start.2) | collective-permute-done | bytes 3145760 | tf_op jit(solution)/shard_map/ppermute | solution.py:41
  635.6 0.0 copy-done
  635.6 0.0 copy-done.1
  635.6 18.8 %convert_add_fusion = f32[768,2048]{1,0:T(8,128)} fusion(bf16[768,2048]{1,0:T(8,128)(2,1)} %collective-permute-done.2, bf16[4096,2048]{1,0:T(8,128)(2,1)} %all-gather.5.cloned.1.call-done, bf16[1536,2048]{1,0:T(8,128)(2,1)S(1)} %copy-done, bf16[1536,2048]{1,0:T(8,128)(2,1)S(1)} %copy-done.1), kind=kOutput, calls=%fused_computation.11 | convolution fusion | flops 12900630528 | bytes 38797312 | tf_op jit(solution)/shard_map/dot_general | solution.py:42
Async XLA Ops:
  6.5 246.0 %all-gather.3.cloned.1.call-start = ((), (), s32[]{:S(2)}) async-start(), calls=%async_computation | async-start | bytes 31457280 | tf_op jit(solution)/shard_map/all_gather | solution.py:35
  6.5 70.0 %collective-permute-start = (bf16[768,2048]{1,0:T(8,128)(2,1)}, bf16[768,2048]{1,0:T(8,128)(2,1)S(1)}, u32[]{:S(2)}, u32[]{:S(2)}) collective-permute-start(bf16[768,2048]{1,0:T(8,128)(2,1)} %param.5), channel_id=1, source_target_pairs={{0,8},{4,12},{8,0},{12,4},{16,24},{20,28},{24,16},{28,20},{1,9},{5... | collective-permute-start | bytes 9437192 | tf_op jit(solution)/shard_map/ppermute | solution.py:27
  7.8 68.0 %collective-permute-start.1 = (s32[768]{0:T(1024)}, s32[768]{0:T(1024)S(1)}, u32[]{:S(2)}, u32[]{:S(2)}) collective-permute-start(s32[768]{0:T(1024)} %param.6), channel_id=1, source_target_pairs={{0,8},{4,12},{8,0},{12,4},{16,24},{20,28},{24,16},{28,20},{1,9},{5... | collective-permute-start | bytes 9224 | tf_op jit(solution)/shard_map/ppermute | solution.py:28
  95.2 448.8 %all-gather.5.cloned.1.call-start = ((), (), s32[]{:S(2)}) async-start(), calls=%async_computation.1 | async-start | bytes 20971520 | tf_op jit(solution)/shard_map/all_gather | solution.py:24
  544.0 91.6 %copy-start = (bf16[1536,2048]{1,0:T(8,128)(2,1)S(1)}, bf16[1536,2048]{1,0:T(8,128)(2,1)}, u32[]{:S(2)}) copy-start(bf16[1536,2048]{1,0:T(8,128)(2,1)} %get-tuple-element.5) | copy-start | bytes 18874372
  544.0 91.6 %copy-start.1 = (bf16[1536,2048]{1,0:T(8,128)(2,1)S(1)}, bf16[1536,2048]{1,0:T(8,128)(2,1)}, u32[]{:S(2)}) copy-start(bf16[1536,2048]{1,0:T(8,128)(2,1)} %get-tuple-element.6) | copy-start | bytes 18874372
  565.0 70.6 %collective-permute-start.2 = (bf16[768,2048]{1,0:T(8,128)(2,1)S(1)}, bf16[768,2048]{1,0:T(8,128)(2,1)}, u32[]{:S(2)}, u32[]{:S(2)}) collective-permute-start(bf16[768,2048]{1,0:T(8,128)(2,1)S(1)} %fusion.8), channel_id=1, source_target_pairs={{0,8},{4,12},{8,0},{12,4},{16,24},{20,28},{24,16},{28,20},{1,9},{5... | collective-permute-start | bytes 9437192 | tf_op jit(solution)/shard_map/ppermute | solution.py:41
Sparse Core Ops, SparseCore 0:
  95.3 157.1 all-gather.2
  254.3 289.6 all-gather.4

commit v2 on v1

--- a/solution.py
+++ b/solution.py
@@ -1,7 +1,13 @@
 import jax
 import jax.numpy as jnp
 from jax import lax
+from jax.experimental import pallas as pl
+from jax.experimental.pallas import tpu as pltpu
 from jax.sharding import PartitionSpec as P
+
+MESH = pl.DeviceIdType.MESH
+CHUNKS = 8
+EARLY = 3
 
 DEPTH = 4
 
@@ -43,11 +49,233 @@
     return mine + arrived.astype(jnp.float32)
 
 
+def body(lib_hbm, lmk_hbm, lmk_count, root_hbm, out, lib, lmk, kern, root, sent, came, load_sem,
+         bits_sem, root_send, root_recv, kern_x, kern_c, kern_recv, half_send, half_recv):
+    i, m = lax.axis_index("lib"), lax.axis_index("lmk")
+    zh, zl, y = lax.div(i, 4), lax.rem(lax.div(i, 2), 2), lax.rem(i, 2)
+    x, core = lax.div(m, 2), lax.rem(m, 2)
+    by_y = (i + 1 - 2 * y, m)
+    by_zl = (i + 2 - 4 * zl, m)
+    by_zh = (i + 4 - 8 * zh, m)
+    by_x = (i, m + 2 - 4 * x)
+    by_core = (i, m + 1 - 2 * core)
+    home = core == zl
+    away = core != zl
+    rows = lib.shape[1]
+    width = root.shape[3] // CHUNKS
+
+    def columns(j):
+        return pl.ds(pl.multiple_of(j * width, width), width)
+
+    def remote(src, dst, send, recv, peer):
+        return pltpu.make_async_remote_copy(
+            src_ref=src, dst_ref=dst, send_sem=send, recv_sem=recv, device_id=peer, device_id_type=MESH
+        )
+
+    def root_copy(way, j, p, q, peer, src=None):
+        dst = root.at[p, q, :, columns(j)]
+        src = dst if src is None else src.at[:, columns(j)]
+        return remote(src, dst, root_send.at[way, j], root_recv.at[way, j], peer)
+
+    def to_y(j):
+        return root_copy(0, j, zh, y, by_y, root_hbm)
+
+    def to_zh(j):
+        return root_copy(1, j, zh, y, by_zh, root_hbm)
+
+    def hand_on(j):
+        return root_copy(2, j, 1 - zh, y, by_y)
+
+    def bits_copy():
+        return remote(lib_hbm, lib.at[1], bits_sem.at[0], bits_sem.at[1], by_zl)
+
+    def kern_to_x(r):
+        return remote(kern.at[x, r], kern.at[x, r], kern_x.at[r], kern_recv.at[x, r], by_x)
+
+    def kern_from_x(r):
+        return remote(kern.at[1 - x, r], kern.at[1 - x, r], kern_x.at[r], kern_recv.at[1 - x, r], by_x)
+
+    def kern_to_core(p, r):
+        return remote(kern.at[p, r], kern.at[p, r], kern_c.at[p, r], kern_recv.at[p, r], by_core)
+
+    def half_copy(j):
+        return remote(
+            sent.at[:, columns(j)], came.at[:, columns(j)], half_send.at[j], half_recv.at[j], by_zl
+        )
+
+    barrier = pltpu.get_barrier_semaphore()
+    for peer in (by_y, by_zl, by_zh, by_x, by_core):
+        pl.semaphore_signal(barrier, inc=1, device_id=peer, device_id_type=MESH)
+    pl.semaphore_wait(barrier, 5)
+
+    @pl.when(away)
+    def _():
+        bits_copy().start()
+
+    @pl.loop(0, CHUNKS)
+    def _(j):
+        to_zh(j).start()
+        to_y(j).start()
+
+    load_root = pltpu.make_async_copy(root_hbm, root.at[zh, y], load_sem.at[0])
+    load_lib = pltpu.make_async_copy(lib_hbm, lib.at[0], load_sem.at[1])
+    load_lmk = pltpu.make_async_copy(lmk_hbm, lmk, load_sem.at[2])
+
+    def tversky_rows(r):
+        ones = jnp.ones((lib.shape[2], 128), jnp.bfloat16)
+        row_count = jnp.dot(lib[r], ones, preferred_element_type=jnp.float32)[:, :1]
+        step = min(256, lmk.shape[0])
+
+        @pl.loop(0, lmk.shape[0] // step)
+        def _(k):
+            at = pl.ds(pl.multiple_of(k * step, step), step)
+            common = lax.dot_general(
+                lib[r], lmk[at, :], (((1,), (1,)), ((), ())), preferred_element_type=jnp.float32
+            )
+            scale_sum = 0.9 * row_count + 0.1 * lmk_count[:, at].astype(jnp.float32)
+            kern[x, r, :, at] = (common / scale_sum).astype(jnp.bfloat16)
+
+        kern_to_x(r).start()
+        kern_to_core(x, r).start()
+
+    @pl.when(home)
+    def _():
+        load_lib.start()
+        load_lmk.start()
+        load_root.start()
+        load_lib.wait()
+        load_lmk.wait()
+        tversky_rows(0)
+        bits_copy().wait_recv()
+        tversky_rows(1)
+
+    @pl.when(away)
+    def _():
+        load_root.start()
+
+    @pl.loop(0, EARLY)
+    def _(j):
+        to_zh(j).wait_recv()
+        hand_on(j).start()
+
+    @pl.when(home)
+    def _():
+        @pl.loop(0, 2)
+        def _(r):
+            kern_from_x(r).wait_recv()
+            kern_to_core(1 - x, r).start()
+
+    @pl.when(away)
+    def _():
+        @pl.loop(0, 2)
+        def _(r):
+            kern_to_core(x, r).wait_recv()
+            kern_to_core(1 - x, r).wait_recv()
+
+    load_root.wait()
+
+    def finish(j):
+        half_copy(j).wait_recv()
+        out[:, columns(j)] += came[:, columns(j)].astype(jnp.float32)
+
+    def half_sum(r, j):
+        depth = 2 * root.shape[2]
+        return sum(
+            jnp.dot(
+                kern[p, r],
+                root[p, :, :, columns(j)].reshape(depth, width),
+                preferred_element_type=jnp.float32,
+            )
+            for p in (0, 1)
+        )
+
+    @pl.loop(0, CHUNKS)
+    def _(j):
+        @pl.when(j >= EARLY)
+        def _():
+            to_zh(j).wait_recv()
+            hand_on(j).start()
+
+        to_y(j).wait_recv()
+        hand_on(j).wait_recv()
+        sent[:, columns(j)] = half_sum(1, j).astype(jnp.bfloat16)
+        half_copy(j).start()
+        out[:, columns(j)] = half_sum(0, j)
+
+        @pl.when(j > 0)
+        def _():
+            finish(j - 1)
+
+    finish(CHUNKS - 1)
+
+    @pl.loop(0, CHUNKS)
+    def _(j):
+        to_y(j).wait_send()
+        to_zh(j).wait_send()
+        hand_on(j).wait_send()
+        half_copy(j).wait_send()
+
+    @pl.when(away)
+    def _():
+        bits_copy().wait_send()
+
+    @pl.when(home)
+    def _():
+        @pl.loop(0, 2)
+        def _(r):
+            kern_to_x(r).wait_send()
+            kern_to_core(x, r).wait_send()
+            kern_to_core(1 - x, r).wait_send()
+
+
+def one_kernel(library_bits, library_count, landmark_bits, landmark_count, inverse_root):
+    del library_count
+    rows, bits = library_bits.shape
+    lmks = landmark_bits.shape[0]
+    depth, cols = inverse_root.shape
+    hbm = pl.BlockSpec(memory_space=pl.ANY)
+    vmem = pl.BlockSpec(memory_space=pltpu.VMEM)
+    dma = pltpu.SemaphoreType.DMA
+    return pl.pallas_call(
+        body,
+        out_shape=jax.ShapeDtypeStruct((rows, cols), jnp.float32),
+        in_specs=[hbm, hbm, vmem, hbm],
+        out_specs=vmem,
+        scratch_shapes=[
+            pltpu.VMEM((2, rows, bits), jnp.bfloat16),
+            pltpu.VMEM((lmks, bits), jnp.bfloat16),
+            pltpu.VMEM((2, 2, rows, lmks), jnp.bfloat16),
+            pltpu.VMEM((2, 2, depth, cols), jnp.bfloat16),
+            pltpu.VMEM((rows, cols), jnp.bfloat16),
+            pltpu.VMEM((rows, cols), jnp.bfloat16),
+            dma((3,)),
+            dma((2,)),
+            dma((3, CHUNKS)),
+            dma((3, CHUNKS)),
+            dma((2,)),
+            dma((2, 2)),
+            dma((2, 2)),
+            dma((CHUNKS,)),
+            dma((CHUNKS,)),
+        ],
+        compiler_params=pltpu.CompilerParams(
+            collective_id=0, has_side_effects=True, vmem_limit_bytes=60 * 1024 * 1024
+        ),
+        cost_estimate=pl.CostEstimate(
+            flops=2 * rows * (lmks * bits + 4 * lmks * cols),
+            bytes_accessed=2 * (rows * bits + lmks * bits + depth * cols) + 4 * rows * cols,
+            transcendentals=0,
+        ),
+    )(library_bits, landmark_bits, landmark_count.reshape(1, lmks), inverse_root)
+
+
 def solution(mesh):
     placed = (P("lib", None), P("lib"), P("lmk", None), P("lmk"), P("lib", "lmk"))
     n_lib, n_lmk = mesh.shape["lib"], mesh.shape["lmk"]
 
     def shards(*blocks):
+        if (n_lib, n_lmk) == (8, 4):
+            return one_kernel(*blocks)
         return split_sum(n_lib, n_lmk, *blocks)
 
     return jax.shard_map(

time: 666 us -> 293 us (0.44)
  waiting for transfers between devices: 570 us -> 0 us
  Pallas kernels: 0 us -> 281 us
  matrix products: 58.5 us -> 0 us
  between operations: 13.5 us -> 0.01 us
  local copies, waits for them, and re-layouts: 14 us -> 6.29 us
    all_gather x2 -> x0, waiting for transfers between devices: 434 us -> none  [the longest x1 277 us: split_sum(): lax.all_gather(inverse_root, 'lib', axis=0, tiled=True, axis_index_groups...]
    pallas_call x0 -> x1, Pallas kernels: none -> 281 us  [one_kernel(): pl.pallas_call(body, out_shape=jax.ShapeDtypeStruct((rows, cols), jnp.flo...]
    ppermute x3 -> x0, waiting for transfers between devices: 135 us -> none  [the longest x1 68.2 us: split_sum(): arrived = lax.ppermute(theirs, 'lib', swap)]
    dot_general x3 -> x0, matrix products: 58.5 us -> none  [the longest x1 21 us: split_sum(): jnp.dot(half[:rows], root, preferred_element_type=jnp.float32)]
    dynamic_slice x1 -> x0, local copies, waits for them, and re-layouts: 14 us -> none  [split_sum(): lax.dynamic_slice_in_dim(kernel, (2 * k + parity) * quarter, quarter, 1)]
  transfers between devices with their start and end apart: 5 -> 0, of which waited for: 4 -> 0; matrix products, arithmetic and copies ran while one was open for 2% -> 0% of each run, Pallas kernels for 0% -> 0%
where the time goes in v2:
time: 293 us; the launch traced here: 288 us
  Pallas kernels  281 us (96%)
  local copies, waits for them, and re-layouts  6.29 us (2%)
    pallas_call x1, Pallas kernels, one_kernel(): pl.pallas_call(body, out_shape=jax.ShapeDtypeStruct((rows, cols), jnp.flo...  281 us
    unnamed x1, local copies, waits for them, and re-layouts  6.29 us

profile of v2, /device:TPU:17, one launch (start us, length us, event | category | flops | bytes accessed | tf_op | source)
XLA Modules:
  0.0 287.6 jit_solution(11579317006722215095)
XLA Ops:
  0.0 281.3 %shard_map.46 = f32[768,2048]{1,0:T(8,128)} custom-call(bf16[768,2048]{1,0:T(8,128)(2,1)} %lib_hbm.1, bf16[2048,2048]{1,0:T(8,128)(2,1)} %lmk_hbm.1, s32[1,2048]{1,0:T(1,128)} %bitcast.1, bf16[1024,2048]{1,0:T(8,128)(2,1)} %root_hbm.1), custom_call_target="tpu_custom_call" | custom-call | flops 32212254720 | bytes 22020096 | tf_op jit(solution)/shard_map/pallas_call | solution.py:239
  281.3 6.3 %copy.6 = f32[768,2048]{1,0:T(8,128)} copy(f32[768,2048]{1,0:T(8,128)} %shard_map.46) | data formatting | bytes 12582912

commit v3 on v2

--- a/solution.py
+++ b/solution.py
@@ -7,6 +7,7 @@
 
 MESH = pl.DeviceIdType.MESH
 CHUNKS = 8
+AHEAD = 2
 EARLY = 3
 
 DEPTH = 4
@@ -112,10 +113,21 @@
     def _():
         bits_copy().start()
 
-    @pl.loop(0, CHUNKS)
+    @pl.loop(0, AHEAD)
     def _(j):
         to_zh(j).start()
         to_y(j).start()
+
+    def serve(j):
+        to_zh(j).wait_recv()
+        hand_on(j).start()
+
+        @pl.when(j + AHEAD < CHUNKS)
+        def _():
+            to_zh(j).wait_send()
+            to_zh(j + AHEAD).start()
+            to_y(j).wait_send()
+            to_y(j + AHEAD).start()
 
     load_root = pltpu.make_async_copy(root_hbm, root.at[zh, y], load_sem.at[0])
     load_lib = pltpu.make_async_copy(lib_hbm, lib.at[0], load_sem.at[1])
@@ -146,8 +158,6 @@
         load_lib.wait()
         load_lmk.wait()
         tversky_rows(0)
-        bits_copy().wait_recv()
-        tversky_rows(1)
 
     @pl.when(away)
     def _():
@@ -155,15 +165,17 @@
 
     @pl.loop(0, EARLY)
     def _(j):
-        to_zh(j).wait_recv()
-        hand_on(j).start()
-
-    @pl.when(home)
-    def _():
-        @pl.loop(0, 2)
-        def _(r):
-            kern_from_x(r).wait_recv()
-            kern_to_core(1 - x, r).start()
+        serve(j)
+
+        @pl.when(home & (j == 0))
+        def _():
+            bits_copy().wait_recv()
+            tversky_rows(1)
+
+        @pl.when(home & (j > 0))
+        def _():
+            kern_from_x(j - 1).wait_recv()
+            kern_to_core(1 - x, j - 1).start()
 
     @pl.when(away)
     def _():
@@ -193,8 +205,7 @@
     def _(j):
         @pl.when(j >= EARLY)
         def _():
-            to_zh(j).wait_recv()
-            hand_on(j).start()
+            serve(j)
 
         to_y(j).wait_recv()
         hand_on(j).wait_recv()
@@ -208,10 +219,13 @@
 
     finish(CHUNKS - 1)
 
-    @pl.loop(0, CHUNKS)
+    @pl.loop(CHUNKS - AHEAD, CHUNKS)
     def _(j):
         to_y(j).wait_send()
         to_zh(j).wait_send()
+
+    @pl.loop(0, CHUNKS)
+    def _(j):
         hand_on(j).wait_send()
         half_copy(j).wait_send()
 

time: 293 us -> 260 us (0.89); the launches traced: 288 us -> 260 us
  Pallas kernels: 281 us -> 254 us
    pallas_call x1, Pallas kernels: 281 us -> 254 us  [one_kernel(): pl.pallas_call(body, out_shape=jax.ShapeDtypeStruct((rows, cols), jnp.flo...]
where the time goes in v3:
time: 260 us
  Pallas kernels  254 us (98%)
  local copies, waits for them, and re-layouts  6.29 us (2%)
    pallas_call x1, Pallas kernels, one_kernel(): pl.pallas_call(body, out_shape=jax.ShapeDtypeStruct((rows, cols), jnp.flo...  254 us
    unnamed x1, local copies, waits for them, and re-layouts  6.29 us

profile of v3, /device:TPU:17, one launch (start us, length us, event | category | flops | bytes accessed | tf_op | source)
XLA Modules:
  0.0 260.1 jit_solution(3108050500363386150)
XLA Ops:
  0.0 253.8 %shard_map.46 = f32[768,2048]{1,0:T(8,128)} custom-call(bf16[768,2048]{1,0:T(8,128)(2,1)} %lib_hbm.1, bf16[2048,2048]{1,0:T(8,128)(2,1)} %lmk_hbm.1, s32[1,2048]{1,0:T(1,128)} %bitcast.1, bf16[1024,2048]{1,0:T(8,128)(2,1)} %root_hbm.1), custom_call_target="tpu_custom_call" | custom-call | flops 32212254720 | bytes 22020096 | tf_op jit(solution)/shard_map/pallas_call | solution.py:253
  253.8 6.3 %copy.6 = f32[768,2048]{1,0:T(8,128)} copy(f32[768,2048]{1,0:T(8,128)} %shard_map.46) | data formatting | bytes 12582912

commit v4 on v3

--- a/solution.py
+++ b/solution.py
@@ -6,9 +6,10 @@
 from jax.sharding import PartitionSpec as P
 
 MESH = pl.DeviceIdType.MESH
-CHUNKS = 8
-AHEAD = 2
-EARLY = 3
+CHUNKS = 16
+AHEAD = 4
+EARLY = 6
+PIECES = 3
 
 DEPTH = 4
 
@@ -63,6 +64,7 @@
     home = core == zl
     away = core != zl
     rows = lib.shape[1]
+    part = rows // PIECES
     width = root.shape[3] // CHUNKS
 
     def columns(j):
@@ -87,17 +89,29 @@
     def hand_on(j):
         return root_copy(2, j, 1 - zh, y, by_y)
 
-    def bits_copy():
-        return remote(lib_hbm, lib.at[1], bits_sem.at[0], bits_sem.at[1], by_zl)
-
-    def kern_to_x(r):
-        return remote(kern.at[x, r], kern.at[x, r], kern_x.at[r], kern_recv.at[x, r], by_x)
-
-    def kern_from_x(r):
-        return remote(kern.at[1 - x, r], kern.at[1 - x, r], kern_x.at[r], kern_recv.at[1 - x, r], by_x)
-
-    def kern_to_core(p, r):
-        return remote(kern.at[p, r], kern.at[p, r], kern_c.at[p, r], kern_recv.at[p, r], by_core)
+    def piece(q):
+        return pl.ds(pl.multiple_of(q * part, part), part)
+
+    def bits_copy(q):
+        return remote(
+            lib_hbm.at[piece(q)], lib.at[1, piece(q)], bits_sem.at[0, q], bits_sem.at[1, q], by_zl
+        )
+
+    def kern_copy(p, r, q, send, peer):
+        at = kern.at[p, r, piece(q)]
+        return remote(at, at, send, kern_recv.at[p, r, q], peer)
+
+    def kern_to_x(r, q):
+        return kern_copy(x, r, q, kern_x.at[r, q], by_x)
+
+    def kern_from_x(r, q):
+        return kern_copy(1 - x, r, q, kern_x.at[r, q], by_x)
+
+    def kern_to_core(p, r, q):
+        return kern_copy(p, r, q, kern_c.at[p, r, q], by_core)
+
+    def each_piece(step):
+        pl.loop(0, PIECES)(step)
 
     def half_copy(j):
         return remote(
@@ -111,7 +125,7 @@
 
     @pl.when(away)
     def _():
-        bits_copy().start()
+        each_piece(lambda q: bits_copy(q).start())
 
     @pl.loop(0, AHEAD)
     def _(j):
@@ -133,22 +147,29 @@
     load_lib = pltpu.make_async_copy(lib_hbm, lib.at[0], load_sem.at[1])
     load_lmk = pltpu.make_async_copy(lmk_hbm, lmk, load_sem.at[2])
 
-    def tversky_rows(r):
+    def tversky_piece(r, q):
         ones = jnp.ones((lib.shape[2], 128), jnp.bfloat16)
-        row_count = jnp.dot(lib[r], ones, preferred_element_type=jnp.float32)[:, :1]
+        row_count = jnp.dot(lib[r, piece(q)], ones, preferred_element_type=jnp.float32)[:, :1]
         step = min(256, lmk.shape[0])
 
         @pl.loop(0, lmk.shape[0] // step)
         def _(k):
             at = pl.ds(pl.multiple_of(k * step, step), step)
             common = lax.dot_general(
-                lib[r], lmk[at, :], (((1,), (1,)), ((), ())), preferred_element_type=jnp.float32
+                lib[r, piece(q)],
+                lmk[at, :],
+                (((1,), (1,)), ((), ())),
+                preferred_element_type=jnp.float32,
             )
             scale_sum = 0.9 * row_count + 0.1 * lmk_count[:, at].astype(jnp.float32)
-            kern[x, r, :, at] = (common / scale_sum).astype(jnp.bfloat16)
-
-        kern_to_x(r).start()
-        kern_to_core(x, r).start()
+            kern[x, r, piece(q), at] = (common / scale_sum).astype(jnp.bfloat16)
+
+        kern_to_x(r, q).start()
+        kern_to_core(x, r, q).start()
+
+    def pass_to_core(r, q):
+        kern_from_x(r, q).wait_recv()
+        kern_to_core(1 - x, r, q).start()
 
     @pl.when(home)
     def _():
@@ -157,7 +178,7 @@
         load_root.start()
         load_lib.wait()
         load_lmk.wait()
-        tversky_rows(0)
+        each_piece(lambda q: tversky_piece(0, q))
 
     @pl.when(away)
     def _():
@@ -167,22 +188,26 @@
     def _(j):
         serve(j)
 
-        @pl.when(home & (j == 0))
-        def _():
-            bits_copy().wait_recv()
-            tversky_rows(1)
-
-        @pl.when(home & (j > 0))
-        def _():
-            kern_from_x(j - 1).wait_recv()
-            kern_to_core(1 - x, j - 1).start()
+        @pl.when(home & (lax.rem(j, 2) == 1))
+        def _():
+            q = lax.div(j, 2)
+            bits_copy(q).wait_recv()
+            tversky_piece(1, q)
+
+        @pl.when(home & (j == 4))
+        def _():
+            each_piece(lambda q: pass_to_core(0, q))
+
+    @pl.when(home)
+    def _():
+        each_piece(lambda q: pass_to_core(1, q))
 
     @pl.when(away)
     def _():
         @pl.loop(0, 2)
         def _(r):
-            kern_to_core(x, r).wait_recv()
-            kern_to_core(1 - x, r).wait_recv()
+            each_piece(lambda q: kern_to_core(x, r, q).wait_recv())
+            each_piece(lambda q: kern_to_core(1 - x, r, q).wait_recv())
 
     load_root.wait()
 
@@ -231,15 +256,15 @@
 
     @pl.when(away)
     def _():
-        bits_copy().wait_send()
+        each_piece(lambda q: bits_copy(q).wait_send())
 
     @pl.when(home)
     def _():
         @pl.loop(0, 2)
         def _(r):
-            kern_to_x(r).wait_send()
-            kern_to_core(x, r).wait_send()
-            kern_to_core(1 - x, r).wait_send()
+            each_piece(lambda q: kern_to_x(r, q).wait_send())
+            each_piece(lambda q: kern_to_core(x, r, q).wait_send())
+            each_piece(lambda q: kern_to_core(1 - x, r, q).wait_send())
 
 
 def one_kernel(library_bits, library_count, landmark_bits, landmark_count, inverse_root):
@@ -263,12 +288,12 @@
             pltpu.VMEM((rows, cols), jnp.bfloat16),
             pltpu.VMEM((rows, cols), jnp.bfloat16),
             dma((3,)),
-            dma((2,)),
+            dma((2, PIECES)),
             dma((3, CHUNKS)),
             dma((3, CHUNKS)),
-            dma((2,)),
-            dma((2, 2)),
-            dma((2, 2)),
+            dma((2, PIECES)),
+            dma((2, 2, PIECES)),
+            dma((2, 2, PIECES)),
             dma((CHUNKS,)),
             dma((CHUNKS,)),
         ],

time: 260 us -> 282 us (1.085); the launches traced: 260 us -> 277 us
  Pallas kernels: 254 us -> 271 us
    pallas_call x1, Pallas kernels: 254 us -> 271 us  [one_kernel(): pl.pallas_call(body, out_shape=jax.ShapeDtypeStruct((rows, cols), jnp.flo...]
where the time goes in v4:
time: 282 us; the launch traced here: 277 us
  Pallas kernels  271 us (96%)
  local copies, waits for them, and re-layouts  6.29 us (2%)
    pallas_call x1, Pallas kernels, one_kernel(): pl.pallas_call(body, out_shape=jax.ShapeDtypeStruct((rows, cols), jnp.flo...  271 us
    unnamed x1, local copies, waits for them, and re-layouts  6.29 us

profile of v4, /device:TPU:17, one launch (start us, length us, event | category | flops | bytes accessed | tf_op | source)
XLA Modules:
  0.0 277.2 jit_solution(17631002713994320161)
XLA Ops:
  0.0 270.9 %shard_map.46 = f32[768,2048]{1,0:T(8,128)} custom-call(bf16[768,2048]{1,0:T(8,128)(2,1)} %lib_hbm.1, bf16[2048,2048]{1,0:T(8,128)(2,1)} %lmk_hbm.1, s32[1,2048]{1,0:T(1,128)} %bitcast.1, bf16[1024,2048]{1,0:T(8,128)(2,1)} %root_hbm.1), custom_call_target="tpu_custom_call" | custom-call | flops 32212254720 | bytes 22020096 | tf_op jit(solution)/shard_map/pallas_call | solution.py:278
  270.9 6.3 %copy.6 = f32[768,2048]{1,0:T(8,128)} copy(f32[768,2048]{1,0:T(8,128)} %shard_map.46) | data formatting | bytes 12582912

commit v5 on v4

--- a/solution.py
+++ b/solution.py
@@ -6,10 +6,10 @@
 from jax.sharding import PartitionSpec as P
 
 MESH = pl.DeviceIdType.MESH
-CHUNKS = 16
-AHEAD = 4
-EARLY = 6
+CHUNKS = 8
+AHEAD = 2
 PIECES = 3
+EARLY = PIECES
 
 DEPTH = 4
 
@@ -51,8 +51,8 @@
     return mine + arrived.astype(jnp.float32)
 
 
-def body(lib_hbm, lmk_hbm, lmk_count, root_hbm, out, lib, lmk, kern, root, sent, came, load_sem,
-         bits_sem, root_send, root_recv, kern_x, kern_c, kern_recv, half_send, half_recv):
+def body(lib_hbm, lmk_hbm, lmk_count, root_hbm, out, lib, lmk, kern, root, sent, came, root_sem,
+         load_sem, bits_sem, root_send, root_recv, kern_x, kern_c, kern_recv, half_send, half_recv):
     i, m = lax.axis_index("lib"), lax.axis_index("lmk")
     zh, zl, y = lax.div(i, 4), lax.rem(lax.div(i, 2), 2), lax.rem(i, 2)
     x, core = lax.div(m, 2), lax.rem(m, 2)
@@ -65,7 +65,7 @@
     away = core != zl
     rows = lib.shape[1]
     part = rows // PIECES
-    width = root.shape[3] // CHUNKS
+    width = root.shape[4]
 
     def columns(j):
         return pl.ds(pl.multiple_of(j * width, width), width)
@@ -75,16 +75,18 @@
             src_ref=src, dst_ref=dst, send_sem=send, recv_sem=recv, device_id=peer, device_id_type=MESH
         )
 
-    def root_copy(way, j, p, q, peer, src=None):
-        dst = root.at[p, q, :, columns(j)]
-        src = dst if src is None else src.at[:, columns(j)]
-        return remote(src, dst, root_send.at[way, j], root_recv.at[way, j], peer)
+    def load_root(j):
+        return pltpu.make_async_copy(root_hbm.at[:, columns(j)], root.at[zh, y, j], root_sem.at[j])
+
+    def root_copy(way, j, p, q, peer):
+        at = root.at[p, q, j]
+        return remote(at, at, root_send.at[way, j], root_recv.at[way, j], peer)
 
     def to_y(j):
-        return root_copy(0, j, zh, y, by_y, root_hbm)
+        return root_copy(0, j, zh, y, by_y)
 
     def to_zh(j):
-        return root_copy(1, j, zh, y, by_zh, root_hbm)
+        return root_copy(1, j, zh, y, by_zh)
 
     def hand_on(j):
         return root_copy(2, j, 1 - zh, y, by_y)
@@ -115,8 +117,20 @@
 
     def half_copy(j):
         return remote(
-            sent.at[:, columns(j)], came.at[:, columns(j)], half_send.at[j], half_recv.at[j], by_zl
+            sent.at[j], came.at[j], half_send.at[j], half_recv.at[j], by_zl
         )
+
+    load_lib = pltpu.make_async_copy(lib_hbm, lib.at[0], load_sem.at[0])
+    load_lmk = pltpu.make_async_copy(lmk_hbm, lmk, load_sem.at[1])
+
+    @pl.loop(0, CHUNKS)
+    def _(j):
+        load_root(j).start()
+
+    @pl.when(home)
+    def _():
+        load_lib.start()
+        load_lmk.start()
 
     barrier = pltpu.get_barrier_semaphore()
     for peer in (by_y, by_zl, by_zh, by_x, by_core):
@@ -129,8 +143,13 @@
 
     @pl.loop(0, AHEAD)
     def _(j):
+        load_root(j).wait()
         to_zh(j).start()
         to_y(j).start()
+
+    @pl.loop(AHEAD, CHUNKS)
+    def _(j):
+        load_root(j).wait()
 
     def serve(j):
         to_zh(j).wait_recv()
@@ -142,10 +161,6 @@
             to_zh(j + AHEAD).start()
             to_y(j).wait_send()
             to_y(j + AHEAD).start()
-
-    load_root = pltpu.make_async_copy(root_hbm, root.at[zh, y], load_sem.at[0])
-    load_lib = pltpu.make_async_copy(lib_hbm, lib.at[0], load_sem.at[1])
-    load_lmk = pltpu.make_async_copy(lmk_hbm, lmk, load_sem.at[2])
 
     def tversky_piece(r, q):
         ones = jnp.ones((lib.shape[2], 128), jnp.bfloat16)
@@ -173,28 +188,20 @@
 
     @pl.when(home)
     def _():
-        load_lib.start()
-        load_lmk.start()
-        load_root.start()
         load_lib.wait()
         load_lmk.wait()
         each_piece(lambda q: tversky_piece(0, q))
 
-    @pl.when(away)
-    def _():
-        load_root.start()
-
     @pl.loop(0, EARLY)
     def _(j):
         serve(j)
 
-        @pl.when(home & (lax.rem(j, 2) == 1))
-        def _():
-            q = lax.div(j, 2)
-            bits_copy(q).wait_recv()
-            tversky_piece(1, q)
-
-        @pl.when(home & (j == 4))
+        @pl.when(home)
+        def _():
+            bits_copy(j).wait_recv()
+            tversky_piece(1, j)
+
+        @pl.when(home & (j == 1))
         def _():
             each_piece(lambda q: pass_to_core(0, q))
 
@@ -209,18 +216,16 @@
             each_piece(lambda q: kern_to_core(x, r, q).wait_recv())
             each_piece(lambda q: kern_to_core(1 - x, r, q).wait_recv())
 
-    load_root.wait()
-
     def finish(j):
         half_copy(j).wait_recv()
-        out[:, columns(j)] += came[:, columns(j)].astype(jnp.float32)
+        out[:, columns(j)] += came[j].astype(jnp.float32)
 
     def half_sum(r, j):
-        depth = 2 * root.shape[2]
+        depth = 2 * root.shape[3]
         return sum(
             jnp.dot(
                 kern[p, r],
-                root[p, :, :, columns(j)].reshape(depth, width),
+                root[p, :, j].reshape(depth, width),
                 preferred_element_type=jnp.float32,
             )
             for p in (0, 1)
@@ -234,7 +239,7 @@
 
         to_y(j).wait_recv()
         hand_on(j).wait_recv()
-        sent[:, columns(j)] = half_sum(1, j).astype(jnp.bfloat16)
+        sent[j] = half_sum(1, j).astype(jnp.bfloat16)
         half_copy(j).start()
         out[:, columns(j)] = half_sum(0, j)
 
@@ -272,6 +277,7 @@
     rows, bits = library_bits.shape
     lmks = landmark_bits.shape[0]
     depth, cols = inverse_root.shape
+    width = cols // CHUNKS
     hbm = pl.BlockSpec(memory_space=pl.ANY)
     vmem = pl.BlockSpec(memory_space=pltpu.VMEM)
     dma = pltpu.SemaphoreType.DMA
@@ -284,10 +290,11 @@
             pltpu.VMEM((2, rows, bits), jnp.bfloat16),
             pltpu.VMEM((lmks, bits), jnp.bfloat16),
             pltpu.VMEM((2, 2, rows, lmks), jnp.bfloat16),
-            pltpu.VMEM((2, 2, depth, cols), jnp.bfloat16),
-            pltpu.VMEM((rows, cols), jnp.bfloat16),
-            pltpu.VMEM((rows, cols), jnp.bfloat16),
-            dma((3,)),
+            pltpu.VMEM((2, 2, CHUNKS, depth, width), jnp.bfloat16),
+            pltpu.VMEM((CHUNKS, rows, width), jnp.bfloat16),
+            pltpu.VMEM((CHUNKS, rows, width), jnp.bfloat16),
+            dma((CHUNKS,)),
+            dma((2,)),
             dma((2, PIECES)),
             dma((3, CHUNKS)),
             dma((3, CHUNKS)),

time: 282 us -> 250 us (0.89)
  Pallas kernels: 271 us -> 239 us
    pallas_call x1, Pallas kernels: 271 us -> 239 us  [one_kernel(): pl.pallas_call(body, out_shape=jax.ShapeDtypeStruct((rows, cols), jnp.flo...]
where the time goes in v5:
time: 250 us; the launch traced here: 245 us
  Pallas kernels  239 us (96%)
  local copies, waits for them, and re-layouts  6.29 us (3%)
    pallas_call x1, Pallas kernels, one_kernel(): pl.pallas_call(body, out_shape=jax.ShapeDtypeStruct((rows, cols), jnp.flo...  239 us
    unnamed x1, local copies, waits for them, and re-layouts  6.29 us

profile of v5, /device:TPU:17, one launch (start us, length us, event | category | flops | bytes accessed | tf_op | source)
XLA Modules:
  0.0 245.4 jit_solution(11429875915849484940)
XLA Ops:
  0.0 239.2 %shard_map.46 = f32[768,2048]{1,0:T(8,128)} custom-call(bf16[768,2048]{1,0:T(8,128)(2,1)} %lib_hbm.1, bf16[2048,2048]{1,0:T(8,128)(2,1)} %lmk_hbm.1, s32[1,2048]{1,0:T(1,128)} %bitcast.1, bf16[1024,2048]{1,0:T(8,128)(2,1)} %root_hbm.1), custom_call_target="tpu_custom_call" | custom-call | flops 32212254720 | bytes 22020096 | tf_op jit(solution)/shard_map/pallas_call | solution.py:284
  239.2 6.3 %copy.6 = f32[768,2048]{1,0:T(8,128)} copy(f32[768,2048]{1,0:T(8,128)} %shard_map.46) | data formatting | bytes 12582912

commit v6 on v5

--- a/solution.py
+++ b/solution.py
@@ -7,9 +7,9 @@
 
 MESH = pl.DeviceIdType.MESH
 CHUNKS = 8
-AHEAD = 2
+AHEAD_Y, AHEAD_Z = 2, 3
 PIECES = 3
-EARLY = PIECES
+EARLY = PIECES + 1
 
 DEPTH = 4
 
@@ -141,26 +141,31 @@
     def _():
         each_piece(lambda q: bits_copy(q).start())
 
-    @pl.loop(0, AHEAD)
+    @pl.loop(0, CHUNKS)
     def _(j):
         load_root(j).wait()
-        to_zh(j).start()
-        to_y(j).start()
-
-    @pl.loop(AHEAD, CHUNKS)
-    def _(j):
-        load_root(j).wait()
+
+        @pl.when(j < AHEAD_Z)
+        def _():
+            to_zh(j).start()
+
+        @pl.when(j < AHEAD_Y)
+        def _():
+            to_y(j).start()
 
     def serve(j):
         to_zh(j).wait_recv()
         hand_on(j).start()
 
-        @pl.when(j + AHEAD < CHUNKS)
+        @pl.when(j + AHEAD_Z < CHUNKS)
         def _():
             to_zh(j).wait_send()
-            to_zh(j + AHEAD).start()
+            to_zh(j + AHEAD_Z).start()
+
+        @pl.when(j + AHEAD_Y < CHUNKS)
+        def _():
             to_y(j).wait_send()
-            to_y(j + AHEAD).start()
+            to_y(j + AHEAD_Y).start()
 
     def tversky_piece(r, q):
         ones = jnp.ones((lib.shape[2], 128), jnp.bfloat16)
@@ -196,7 +201,7 @@
     def _(j):
         serve(j)
 
-        @pl.when(home)
+        @pl.when(home & (j < PIECES))
         def _():
             bits_copy(j).wait_recv()
             tversky_piece(1, j)
@@ -233,9 +238,9 @@
 
     @pl.loop(0, CHUNKS)
     def _(j):
-        @pl.when(j >= EARLY)
-        def _():
-            serve(j)
+        @pl.when((j + 1 >= EARLY) & (j + 1 < CHUNKS))
+        def _():
+            serve(j + 1)
 
         to_y(j).wait_recv()
         hand_on(j).wait_recv()
@@ -249,9 +254,12 @@
 
     finish(CHUNKS - 1)
 
-    @pl.loop(CHUNKS - AHEAD, CHUNKS)
+    @pl.loop(CHUNKS - AHEAD_Y, CHUNKS)
     def _(j):
         to_y(j).wait_send()
+
+    @pl.loop(CHUNKS - AHEAD_Z, CHUNKS)
+    def _(j):
         to_zh(j).wait_send()
 
     @pl.loop(0, CHUNKS)

time: 250 us -> 269 us (1.076)
  Pallas kernels: 239 us -> 261 us
    pallas_call x1, Pallas kernels: 239 us -> 261 us  [one_kernel(): pl.pallas_call(body, out_shape=jax.ShapeDtypeStruct((rows, cols), jnp.flo...]
where the time goes in v6:
time: 269 us; the launch traced here: 267 us
  Pallas kernels  261 us (97%)
  local copies, waits for them, and re-layouts  6.29 us (2%)
    pallas_call x1, Pallas kernels, one_kernel(): pl.pallas_call(body, out_shape=jax.ShapeDtypeStruct((rows, cols), jnp.flo...  261 us
    unnamed x1, local copies, waits for them, and re-layouts  6.29 us

profile of v6, /device:TPU:17, one launch (start us, length us, event | category | flops | bytes accessed | tf_op | source)
XLA Modules:
  0.0 266.9 jit_solution(609750524843333317)
XLA Ops:
  0.0 260.6 %shard_map.46 = f32[768,2048]{1,0:T(8,128)} custom-call(bf16[768,2048]{1,0:T(8,128)(2,1)} %lib_hbm.1, bf16[2048,2048]{1,0:T(8,128)(2,1)} %lmk_hbm.1, s32[1,2048]{1,0:T(1,128)} %bitcast.1, bf16[1024,2048]{1,0:T(8,128)(2,1)} %root_hbm.1), custom_call_target="tpu_custom_call" | custom-call | flops 32212254720 | bytes 22020096 | tf_op jit(solution)/shard_map/pallas_call | solution.py:292
  260.7 6.3 %copy.6 = f32[768,2048]{1,0:T(8,128)} copy(f32[768,2048]{1,0:T(8,128)} %shard_map.46) | data formatting | bytes 12582912

commit v7 on v6

--- a/solution.py
+++ b/solution.py
@@ -7,9 +7,9 @@
 
 MESH = pl.DeviceIdType.MESH
 CHUNKS = 8
-AHEAD_Y, AHEAD_Z = 2, 3
+AHEAD_Y, AHEAD_Z = 1, 2
 PIECES = 3
-EARLY = PIECES + 1
+EARLY = PIECES
 
 DEPTH = 4
 
@@ -238,9 +238,9 @@
 
     @pl.loop(0, CHUNKS)
     def _(j):
-        @pl.when((j + 1 >= EARLY) & (j + 1 < CHUNKS))
-        def _():
-            serve(j + 1)
+        @pl.when(j >= EARLY)
+        def _():
+            serve(j)
 
         to_y(j).wait_recv()
         hand_on(j).wait_recv()

time: 269 us -> 255 us (0.948)
  Pallas kernels: 261 us -> 247 us
    pallas_call x1, Pallas kernels: 261 us -> 247 us  [one_kernel(): pl.pallas_call(body, out_shape=jax.ShapeDtypeStruct((rows, cols), jnp.flo...]
where the time goes in v7:
time: 255 us; the launch traced here: 253 us
  Pallas kernels  247 us (97%)
  local copies, waits for them, and re-layouts  6.29 us (2%)
    pallas_call x1, Pallas kernels, one_kernel(): pl.pallas_call(body, out_shape=jax.ShapeDtypeStruct((rows, cols), jnp.flo...  247 us
    unnamed x1, local copies, waits for them, and re-layouts  6.29 us

profile of v7, /device:TPU:17, one launch (start us, length us, event | category | flops | bytes accessed | tf_op | source)
XLA Modules:
  0.0 253.4 jit_solution(13119558075419368298)
XLA Ops:
  0.0 247.1 %shard_map.46 = f32[768,2048]{1,0:T(8,128)} custom-call(bf16[768,2048]{1,0:T(8,128)(2,1)} %lib_hbm.1, bf16[2048,2048]{1,0:T(8,128)(2,1)} %lmk_hbm.1, s32[1,2048]{1,0:T(1,128)} %bitcast.1, bf16[1024,2048]{1,0:T(8,128)(2,1)} %root_hbm.1), custom_call_target="tpu_custom_call" | custom-call | flops 32212254720 | bytes 22020096 | tf_op jit(solution)/shard_map/pallas_call | solution.py:292
  247.1 6.3 %copy.6 = f32[768,2048]{1,0:T(8,128)} copy(f32[768,2048]{1,0:T(8,128)} %shard_map.46) | data formatting | bytes 12582912
